TPU v7x, 256 devices: a whole 4x4x8 slice. The times are simulated.
256 devices in a mesh: dp: 16 (over y, z_lo), block: 16 (over x, z_hi, core).
Axes of the slice: x: 4, y: 4, z: 8 (z_hi: 2, z_lo: 4; z = z_hi * 4 + z_lo), core: 2. Of those that a mesh axis runs over, the one named last changes fastest.
Arguments:
- grads: float32 [16, 16, 1024, 1024], P('dp', 'block'), may hold values from -0.15625 to 0.15625
- owner: int32 [16], replicated, may hold values from 0 to 15, as said below
- stats: float32 [16, 16, 512, 1024], P('block', 'dp'), as said below
Outputs:
- new_stats: float32 [16, 16, 512, 1024], P('block', 'dp')
- roots: float32 [16, 2, 1024, 1024], P('block', None, 'dp')
Inputs may be any that keep to these rules, and one draw needn't show every extreme that they name: No owner has more than 4 blocks, and some owner has exactly 4. `stats`: each statistic matrix assembled from the row halves is symmetric.
All inputs are finite; a program needn't handle non-finite values.
Results may differ from a plain program's by a relative error of at most 0.0003.
Values sent between devices are 32-bit elements; how exact they have to be, the bound alone decides.
A program may use at most 128 MiB of HBM per device.

v0:
```python
import jax
import jax.numpy as jnp
from jax import lax
from jax.sharding import PartitionSpec as P

PSTEPS = 8


stat_decay = 0.6


def swapped(array, axis, distance):
    return lax.ppermute(array, axis, [(i, i ^ 1 << distance) for i in range(lax.axis_size(axis))])


def product(left_side, right_side):
    return jnp.dot(left_side, right_side, precision=lax.Precision.HIGHEST)


def assemble(own_part, other_part, lower_half):
    first_part = jnp.where(lower_half, own_part, other_part)
    second_part = jnp.where(lower_half, other_part, own_part)
    return jnp.concatenate([first_part, second_part], axis=0)


def owner_buffer(pieces, ranking, owned_mask, slot_count):
    clipped = jnp.clip(ranking, 0, slot_count - 1)
    return (
        jnp.take(pieces, clipped, axis=0)
        * owned_mask.astype(jnp.float32)[:, None, None, None, None]
    )


def per_device(grads, owner, stats):
    dp_count = lax.axis_size("dp")
    block_count = lax.axis_size("block")
    per_shard = grads.shape[1]
    block_order = grads.shape[2]
    slab_rows = block_order // dp_count
    half_order = block_order // 2
    slot_count = dp_count // 4
    dp_index = lax.axis_index("dp")
    block_index = lax.axis_index("block")
    reduced = lax.psum_scatter(grads[0], "dp", scatter_dimension=1, tiled=True)
    everywhere = lax.all_gather(reduced, "block", axis=0, tiled=True)
    total_blocks = per_shard * block_count
    block_ids = jnp.arange(total_blocks, dtype=jnp.int32)
    slot_ids = jnp.arange(slot_count, dtype=jnp.int32)
    owned_mask = (owner == block_index).astype(jnp.int32)
    ranking = jnp.cumsum(owned_mask) - 1
    matched = (owned_mask[None, :] == 1) & (ranking[None, :] == slot_ids[:, None])
    chosen = jnp.sum(jnp.where(matched, block_ids[None, :], 0), axis=1)
    present = jnp.any(matched, axis=1).astype(jnp.float32)
    picked = jnp.take(everywhere, chosen, axis=0) * present[:, None, None]
    outgoing = jnp.repeat(picked, 4, axis=0)
    incoming = lax.all_to_all(outgoing, "dp", split_axis=0, concat_axis=0, tiled=True)
    gradient = incoming.reshape(block_order, block_order)
    stat_kind = dp_index // 2 % 2
    upper_half = dp_index % 2
    lower_half = upper_half == 0
    oriented = jnp.where(stat_kind == 0, gradient, gradient.T)
    own_rows = lax.dynamic_slice_in_dim(oriented, upper_half * half_order, half_order, 0)
    gram_rows = lax.dot_general(
        own_rows, oriented, (((1,), (1,)), ((), ())), precision=lax.Precision.HIGHEST
    )
    stat_rows = stat_decay * stats[0, 0] + (1.0 - stat_decay) * gram_rows
    other_rows = swapped(stat_rows, "dp", 0)
    statistic = assemble(stat_rows, other_rows, lower_half)
    probe = jnp.full((block_order,), block_order ** (-0.5), jnp.float32)
    for power_step in range(PSTEPS):
        image = product(statistic, probe)
        probe = image / jnp.sqrt(jnp.sum(image * image))
    final_image = product(statistic, probe)
    top_value = jnp.sqrt(jnp.sum(final_image * final_image))
    scale_value = 2.5 / top_value
    scaled = scale_value * statistic
    identity = jnp.eye(block_order, dtype=jnp.float32)
    first_step = (5.0 * identity - scaled) / 4.0
    iterate = first_step * scale_value**0.25
    step_rows = lax.dynamic_slice_in_dim(first_step, upper_half * half_order, half_order, 0)
    square_rows = product(step_rows, first_step)
    square_term = assemble(square_rows, swapped(square_rows, "dp", 0), lower_half)
    fourth_rows = product(square_rows, square_term)
    updated_rows = product(fourth_rows, scaled)
    identity_rows = lax.dynamic_slice_in_dim(identity, upper_half * half_order, half_order, 0)
    next_rows = (5.0 * identity_rows - updated_rows) / 4.0
    second_step = assemble(next_rows, swapped(next_rows, "dp", 0), lower_half)
    step_columns = lax.dynamic_slice_in_dim(second_step, upper_half * half_order, half_order, 1)
    root_columns = product(iterate, step_columns)
    spread = lax.all_to_all(
        root_columns.reshape(dp_count, slab_rows, half_order),
        "dp",
        split_axis=0,
        concat_axis=0,
        tiled=True,
    )
    pieces = spread.reshape(slot_count, 2, 2, slab_rows, half_order)
    outgoing_blocks = owner_buffer(pieces, ranking, owned_mask, slot_count)
    mine_blocks = lax.psum_scatter(outgoing_blocks, "block", scatter_dimension=0, tiled=True)
    root_blocks = mine_blocks.transpose(0, 1, 3, 2, 4).reshape(per_shard, 2, slab_rows, block_order)
    return (stat_rows[None, None], root_blocks)


def solution(mesh):
    return jax.shard_map(
        per_device,
        mesh=mesh,
        in_specs=(P("dp", "block", None, None), P(), P("block", "dp", None, None)),
        out_specs=(P("block", "dp", None, None), P("block", None, "dp", None)),
        check_vma=False,
    )
```

profile of v0, /device:TPU:4, one launch (start us, length us, event | category | flops | bytes accessed | tf_op | source)
XLA Modules:
  0.0 766.3 jit_solution(14263735600629281940)
XLA Ops:
  7.2 0.0 reduce-scatter.3.cloned.1.call-start
  7.2 0.0 copy-start.5
  7.2 0.7 reduce-scatter.3.cloned.1.call-update
  7.9 0.0 all-gather.2.cloned.1.call-start
  7.9 109.2 %reduce-scatter.3.cloned.1.call-done = f32[1,64,1024]{2,1,0:T(8,128)} async-done(((f32[1,1024,1024]{2,1,0:T(8,128)}), f32[1,64,1024]{2,1,0:T(8,128)}) %reduce-scatter.3.cloned.1.call-update) | async-done | bytes 262160 | tf_op jit(solution)/shard_map/reduce_scatter | solution.py:44
  117.1 0.0 all-gather.2.cloned.1.call-update
  117.2 0.1 copy.16
  117.3 0.1 fusion.24
  117.4 0.1 fusion.31
  117.6 0.1 select_reduce_fusion
  117.7 74.6 %all-gather.2.cloned.1.call-done = f32[16,64,1024]{2,1,0:T(8,128)} async-done(((f32[1,64,1024]{2,1,0:T(8,128)}), f32[16,64,1024]{2,1,0:T(8,128)}) %all-gather.2.cloned.1.call-update) | async-done | bytes 4194320 | tf_op jit(solution)/shard_map/all_gather | solution.py:45
  192.3 2.8 gather_fusion
  195.1 0.2 select_multiply_fusion.1
  195.3 2.5 broadcast_in_dim.51
  197.8 4.5 all-to-all-start
  202.4 97.2 %all-to-all-done = f32[16,64,1024]{2,1,0:T(8,128)} async-done(((f32[16,64,1024]{2,1,0:T(8,128)}), f32[16,64,1024]{2,1,0:T(8,128)}, u32[]{:S(2)}, u32[]{:S(2)}) %all-to-all-start) | async-done | bytes 4194336 | tf_op jit(solution)/shard_map/all_to_all | solution.py:56
  299.6 5.3 copy.17
  304.9 4.5 bitcast_select_fusion
  309.5 0.0 copy-done.4
  309.5 7.1 bitcast_add_fusion
  316.6 0.0 copy-start.3
  316.6 0.3 collective-permute-start
  316.9 1.0 copy-done.3
  317.9 46.0 %collective-permute-done = f32[512,1024]{1,0:T(8,128)} collective-permute-done((f32[512,1024]{1,0:T(8,128)S(1)}, f32[512,1024]{1,0:T(8,128)}, u32[]{:S(2)}, u32[]{:S(2)}) %collective-permute-start) | collective-permute-done | bytes 2097184 | tf_op jit(solution)/shard_map/ppermute | solution.py:13
  363.9 2.7 broadcast_select_fusion.5
  366.6 3.6 fusion.25
  370.2 0.6 multiply_reduce_fusion.8
  371.6 5.2 fusion.47
  376.7 0.6 multiply_reduce_fusion.7
  378.1 5.2 fusion.46
  383.2 0.6 multiply_reduce_fusion.6
  384.6 5.2 fusion.45
  389.7 0.6 multiply_reduce_fusion.5
  391.1 5.6 fusion.44
  396.6 0.6 multiply_reduce_fusion.4
  398.0 5.2 fusion.43
  403.2 0.6 multiply_reduce_fusion.3
  404.5 5.2 fusion.42
  409.7 0.6 multiply_reduce_fusion.2
  411.0 5.2 fusion.41
  416.2 0.6 multiply_reduce_fusion.1
  417.5 5.3 fusion.40
  422.8 0.6 multiply_reduce_fusion
  424.1 2.2 fusion.8
  426.3 6.9 fusion.11
  433.2 0.6 collective-permute-start.1
  433.8 0.3 iota_compare_fusion
  434.1 45.4 %collective-permute-done.1 = f32[512,1024]{1,0:T(8,128)S(1)} collective-permute-done((f32[512,1024]{1,0:T(8,128)S(1)}, f32[512,1024]{1,0:T(8,128)S(1)}, u32[]{:S(2)}, u32[]{:S(2)}) %collective-permute-start.1) | collective-permute-done | bytes 2097184 | tf_op jit(solution)/shard_map/ppermute | solution.py:13
  479.6 0.8 broadcast_select_fusion.3
  480.4 6.9 fusion
  487.4 8.6 %subtract_multiply_fusion = f32[512,1024]{1,0:T(8,128)} fusion(pred[1024,1024]{1,0:T(32,128)(4,1)S(1)} %iota_compare_fusion, s32[]{:T(128)S(6)} %select_n.110, f32[512,1024]{1,0:T(8,128)S(1)} %fusion, f32[]{:T(128)S(6)} %div.90, f32[512,1024]{1,0:T(8,128)S(1)} %copy-done.1, f32[512,1024]{1,0:T(8,128)S(1)} %get-tuple-element.8), kind=kOutput, calls=%fused_computation.20 | convolution fusion | flops 6446645248 | bytes 8912904 | tf_op jit(solution)/shard_map/dot_general | solution.py:17
  495.9 0.6 collective-permute-start.2
  496.6 44.8 %collective-permute-done.2 = f32[512,1024]{1,0:T(8,128)} collective-permute-done((f32[512,1024]{1,0:T(8,128)}, f32[512,1024]{1,0:T(8,128)}, u32[]{:S(2)}, u32[]{:S(2)}) %collective-permute-start.2) | collective-permute-done | bytes 2097184 | tf_op jit(solution)/shard_map/ppermute | solution.py:13
  541.3 3.1 broadcast_select_fusion
  544.4 0.0 copy-done.2
  544.4 8.4 %fusion.4 = f32[1024,512]{1,0:T(8,128)} fusion(s32[]{:T(128)S(6)} %select_n.110, f32[512,1024]{1,0:T(8,128)S(1)} %get-tuple-element.5, f32[512,1024]{1,0:T(8,128)S(1)} %get-tuple-element.4, f32[]{:T(128)S(6)} %mul.111, f32[]{:T(128)S(6)} %div.90, f32[512,1024]{1,0:T(8,128)S(1)} %copy-done.2, f32[512,1024]{1,0:T(8,128)S(1)} %get-tuple-element.8), kind=kOutput, calls=%fused_computation.11 | convolution fusion | flops 6449266688 | bytes 10485772 | tf_op jit(solution)/shard_map/dot_general | solution.py:17
  552.8 5.6 all-to-all-start.1
  558.4 0.0 reduce-scatter.5.cloned.1.call-start
  558.5 47.8 %all-to-all-done.1 = f32[16,64,512]{2,1,0:T(8,128)S(1)} async-done(((f32[16,64,512]{2,1,0:T(8,128)}), f32[16,64,512]{2,1,0:T(8,128)S(1)}, u32[]{:S(2)}, u32[]{:S(2)}) %all-to-all-start.1) | async-done | bytes 2097184 | tf_op jit(solution)/shard_map/all_to_all | solution.py:90
  606.3 4.3 gather_fusion.1
  610.6 8.5 %select_multiply_fusion = f32[16,2,2,64,512]{4,3,2,1,0:T(8,128)} fusion(f32[16,2,2,64,512]{4,3,2,1,0:T(8,128)} %gather_fusion.1, f32[16]{0:T(128)S(1)} %get-tuple-element.10, pred[16]{0:T(512)(128)(4,1)S(1)} %compare_and_fusion), kind=kLoop, calls=%fused_computation.2 | loop fusion | flops 4194304 | bytes 16777296 | tf_op jit(solution)/shard_map/mul | solution.py:29
  619.1 0.0 reduce-scatter.5.cloned.1.call-update
  619.2 138.3 %reduce-scatter.5.cloned.1.call-done = f32[1,2,2,64,512]{4,3,2,1,0:T(8,128)} async-done(((f32[16,2,2,64,512]{4,3,2,1,0:T(8,128)}), f32[1,2,2,64,512]{4,3,2,1,0:T(8,128)}) %reduce-scatter.5.cloned.1.call-update) | async-done | bytes 524304 | tf_op jit(solution)/shard_map/reduce_scatter | solution.py:99
  757.4 1.9 copy.19
  (23 shorter events, 0.1 us)
Async XLA Ops:
  7.2 110.0 %reduce-scatter.3.cloned.1.call-start = ((), (), s32[]{:S(2)}) async-start(), calls=%async_computation.4 | async-start | bytes 4456448 | tf_op jit(solution)/shard_map/reduce_scatter | solution.py:44
  7.2 110.0 %copy-start.5 = (s32[16]{0:T(128)S(1)}, s32[16]{0:T(128)}, u32[]{:S(2)}) copy-start(s32[16]{0:T(128)} %param.4) | copy-start | bytes 196
  7.9 184.4 %all-gather.2.cloned.1.call-start = ((), (), s32[]{:S(2)}) async-start(), calls=%async_computation.5 | async-start | bytes 4456448 | tf_op jit(solution)/shard_map/all_gather | solution.py:45
  197.8 101.7 %all-to-all-start = ((f32[16,64,1024]{2,1,0:T(8,128)}), f32[16,64,1024]{2,1,0:T(8,128)}, u32[]{:S(2)}, u32[]{:S(2)}) async-start(f32[16,64,1024]{2,1,0:T(8,128)} %bitcast.50), calls=%async_computation.1 | async-start | bytes 8388608 | tf_op jit(solution)/shard_map/all_to_all | solution.py:56
  304.9 4.5 copy-start.4
  316.6 1.3 copy-start.3
  316.6 47.4 %collective-permute-start = (f32[512,1024]{1,0:T(8,128)S(1)}, f32[512,1024]{1,0:T(8,128)}, u32[]{:S(2)}, u32[]{:S(2)}) collective-permute-start(f32[512,1024]{1,0:T(8,128)S(1)} %bitcast_add_fusion), channel_id=1, source_target_pairs={{0,16},{16,0},{32,48},{48,32},{64,80},{80,64},{96,112},{112,96},{1... | collective-permute-start | bytes 6291464 | tf_op jit(solution)/shard_map/ppermute | solution.py:13
  366.6 3.6 copy-start
  433.2 46.3 %collective-permute-start.1 = (f32[512,1024]{1,0:T(8,128)S(1)}, f32[512,1024]{1,0:T(8,128)S(1)}, u32[]{:S(2)}, u32[]{:S(2)}) collective-permute-start(f32[512,1024]{1,0:T(8,128)S(1)} %fusion.11), channel_id=1, source_target_pairs={{0,16},{16,0},{32,48},{48,32},{64,80},{80,64},{96,112},{112,96},{1... | collective-permute-start | bytes 6291464 | tf_op jit(solution)/shard_map/ppermute | solution.py:13
  480.4 6.9 copy-start.1
  495.9 45.4 %collective-permute-start.2 = (f32[512,1024]{1,0:T(8,128)}, f32[512,1024]{1,0:T(8,128)}, u32[]{:S(2)}, u32[]{:S(2)}) collective-permute-start(f32[512,1024]{1,0:T(8,128)} %subtract_multiply_fusion), channel_id=1, source_target_pairs={{0,16},{16,0},{32,48},{48,32},{64,80},{80,64},{96,112},{112,96},{1... | collective-permute-start | bytes 6291464 | tf_op jit(solution)/shard_map/ppermute | solution.py:13
  496.6 47.8 %copy-start.2 = (f32[512,1024]{1,0:T(8,128)S(1)}, f32[512,1024]{1,0:T(8,128)}, u32[]{:S(2)}) copy-start(f32[512,1024]{1,0:T(8,128)} %copy-done) | copy-start | bytes 6291460
  552.8 53.5 %all-to-all-start.1 = ((f32[16,64,512]{2,1,0:T(8,128)}), f32[16,64,512]{2,1,0:T(8,128)S(1)}, u32[]{:S(2)}, u32[]{:S(2)}) async-start(f32[16,64,512]{2,1,0:T(8,128)} %bitcast.53), calls=%async_computation.2 | async-start | bytes 4194304 | tf_op jit(solution)/shard_map/all_to_all | solution.py:90
  558.4 199.1 %reduce-scatter.5.cloned.1.call-start = ((), (), s32[]{:S(2)}) async-start(), calls=%async_computation.6 | async-start | bytes 8912896 | tf_op jit(solution)/shard_map/reduce_scatter | solution.py:99
Sparse Core Ops, SparseCore 0:
  10.5 106.5 reduce-scatter.2
  119.8 72.4 all-gather.1
  619.3 138.1 reduce-scatter.4
where the time goes:
time: 776 us; the launch traced here: 766 us
  waiting for transfers between devices  604 us (78%)
  matrix products  83.5 us (11%)
  other arithmetic  28.3 us (4%)
  between operations  20.8 us (3%)
  local copies, waits for them, and re-layouts  17.9 us (2%)
  starting transfers between devices  11.7 us (2%)
    reduce_scatter x1, waiting for transfers between devices, per_device(): lax.psum_scatter(outgoing_blocks, 'block', scatter_dimension=0, tiled=True)  138 us
    ppermute x3, waiting for transfers between devices, swapped(): lax.ppermute(array, axis, [(i, i ^ 1 << distance) for i in range(lax.axis...  136 us
    reduce_scatter x1, waiting for transfers between devices, per_device(): reduced = lax.psum_scatter(grads[0], 'dp', scatter_dimension=1, tiled=True)  109 us
    all_to_all x1, waiting for transfers between devices, per_device(): lax.all_to_all(outgoing, 'dp', split_axis=0, concat_axis=0, tiled=True)  97.2 us
    dot_general x13, matrix products, product(): return jnp.dot(left_side, right_side, precision=lax.Precision.HIGHEST)  76.4 us
    all_gather x1, waiting for transfers between devices, per_device(): everywhere = lax.all_gather(reduced, 'block', axis=0, tiled=True)  74.6 us
    all_to_all x1, waiting for transfers between devices, per_device(): lax.all_to_all(root_columns.reshape(dp_count, slab_rows, half_order), 'dp...  47.8 us
  transfers between devices with their start and end apart: 8, of which 8 were waited for; matrix products, arithmetic and copies ran while one was open for 0% of the time, Pallas kernels for 0%

commit v1 on v0

v1 whole, which is shorter than its diff:
```python
import jax
import jax.numpy as jnp
from jax import lax
from jax.experimental import pallas as pl
from jax.experimental.pallas import tpu as pltpu
from jax.sharding import PartitionSpec as P

PSTEPS = 8
BS = 1024
GROUPS = 2
SUB = 64 // GROUPS
MESH = pl.DeviceIdType.MESH
VMEM_LIMIT = 60 * 1024 * 1024

PACKED = (
    ((0, 0), (0, 1), (1, 1), (0, 2), (0, 3)),
    ((2, 2), (2, 3), (3, 3), (2, 1), (3, 1)),
)


def place(dp, block):
    return dp // 4, dp % 4, block // 4, block // 2 % 2, block % 2


class Network:
    def __init__(self, send, recv, local):
        self.send, self.recv, self.local = send, recv, local
        self.count = self.locals = 0
        self.sent = []
        self.dp, self.block = lax.axis_index("dp"), lax.axis_index("block")
        self.y, self.zl, self.x, self.zh, self.c = place(self.dp, self.block)

    def device(self, y=0, zl=0, x=0, zh=0, c=0, half=0, side=0):
        row = (self.zl + zl) % 4
        if half:
            row = row + 1 - 2 * (row % 2)
        if side:
            row = (row + 2) % 4
        return (
            (self.y + y) % 4 * 4 + row,
            (self.x + x) % 4 * 4 + (self.zh + zh) % 2 * 2 + (self.c + c) % 2,
        )

    def greet(self, steps):
        barrier = pltpu.get_barrier_semaphore()
        for step in steps:
            pl.semaphore_signal(barrier, inc=1, device_id=self.device(**step), device_id_type=MESH)
        pl.semaphore_wait(barrier, len(steps))

    def push(self, source, target, **step):
        n = self.count
        self.count += 1
        copy = pltpu.make_async_remote_copy(
            src_ref=source,
            dst_ref=target,
            send_sem=self.send.at[n],
            recv_sem=self.recv.at[n],
            device_id=self.device(**step),
            device_id_type=MESH,
        )
        copy.start()
        self.sent.append(copy)
        return copy

    def move(self, source, target):
        copy = pltpu.make_async_copy(source, target, self.local.at[self.locals])
        self.locals += 1
        copy.start()
        return copy

    def close(self):
        for copy in self.sent:
            copy.wait_send()


def split(values):
    high = values.astype(jnp.bfloat16)
    return high, (values - high.astype(jnp.float32)).astype(jnp.bfloat16)


def rank_of(owner, block):
    mine = owner[block]
    count = lax.fori_loop(
        0, 16, lambda i, n: n + jnp.where((i < block) & (owner[i] == mine), 1, 0), jnp.int32(0)
    )
    return mine, count


def block_at(owner, column, wanted):
    def step(i, carry):
        count, found, source = carry
        hit = owner[i] == column
        here = hit & (count == wanted)
        return count + jnp.where(hit, 1, 0), jnp.where(here, 1, found), jnp.where(here, i, source)

    zero = jnp.int32(0)
    _, found, source = lax.fori_loop(0, 16, step, (zero, zero, zero))
    return found, source


def find_root(spot, stat, root, column, base, high, low):
    y, zl = spot

    def to_column(row):
        @pl.loop(0, 8)
        def _(i):
            rows = pl.ds(pl.multiple_of(i * 128, 128), 128)
            column[rows, :] = jnp.sum(stat[rows, :] * row, axis=1, keepdims=True)

        return column[...]

    def to_row(values):
        column[...] = values

        def body(i, total):
            rows = pl.ds(pl.multiple_of(i * 128, 128), 128)
            return total + jnp.sum(stat[rows, :] * column[rows, :], axis=0, keepdims=True)

        return lax.fori_loop(0, 8, body, jnp.zeros((1, BS), jnp.float32))

    row = jnp.full((1, BS), BS ** (-0.5), jnp.float32)
    for _ in range(PSTEPS // 2):
        image = to_column(row)
        image = image / jnp.sqrt(jnp.sum(image * image))
        row = to_row(image)
        row = row / jnp.sqrt(jnp.sum(row * row))
    image = to_column(row)
    top = jnp.sqrt(jnp.sum(image * image, axis=(0, 1), keepdims=True))
    scale = 2.5 / top
    fourth = jnp.sqrt(jnp.sqrt(scale))

    @pl.loop(0, 4)
    def _(i):
        rows = pl.ds(pl.multiple_of(i * 256, 256), 256)
        eye = lax.broadcasted_iota(jnp.int32, (256, BS), 0) + i * 256 == lax.broadcasted_iota(
            jnp.int32, (256, BS), 1
        )
        values = (jnp.where(eye, 5.0, 0.0) - scale * stat[rows, :]) / 4.0
        base[rows, :] = values
        upper, lower = split(values)
        high[rows, :] = upper
        low[rows, :] = lower

    def times(left):
        upper, lower = split(left)

        def product(a, b):
            return jnp.dot(a, b, preferred_element_type=jnp.float32)

        both = product(jnp.concatenate([upper, lower], axis=0), high[...])
        return both[128:] + product(upper, low[...]) + both[:128]

    own = pl.multiple_of((y * 4 + zl) * 64, 64)
    other = pl.multiple_of((y * 4 + (zl + 2) % 4) * 64, 64)
    first = jnp.concatenate([base[pl.ds(own, 64), :], base[pl.ds(other, 64), :]], axis=0)
    power = times(times(times(first)))
    result = (5.0 * first + times(4.0 * times(power) - 5.0 * power)) * (fourth / 4.0)
    root[0] = result[:64]
    root[1] = result[64:]


def refresh_kernel(owner, grads, old, parts, crossed, roots, *scratch):
    (far, up, down, toward, away, home, stage, mine, zgot) = scratch[:9]
    (packed, slots, spread, outgo, income, near, cross, fin, oldp) = scratch[9:18]
    (both, chunk, gram, ggot, sall, stat, column, base, rootbuf) = scratch[18:27]
    (columns, leave, enter, ready, piece) = scratch[27:32]
    (mat_high, mat_low, high, low) = scratch[32:36]
    net = Network(*scratch[36:])
    y, zl, x, zh, c = net.y, net.zl, net.x, net.zh, net.c
    side, half = zl // 2, zl % 2
    below, above, beyond = (y + 3) % 4, (y + 1) % 4, (y + 2) % 4

    def rows_of(at, size):
        return pl.ds(pl.multiple_of(at * size, size), size)

    def strip(ref, chunk_at, first, group):
        return ref.at[chunk_at, pl.ds(first, 2), pl.ds(group * SUB, SUB)]

    fetched = []
    for n in range(5):
        i = jnp.where(half == 0, PACKED[0][n][0], PACKED[1][n][0] - 2)
        j = jnp.where(half == 0, PACKED[0][n][1], PACKED[1][n][1])
        fetched.append(net.move(old.at[rows_of(i, 256), rows_of(j, 256)], packed.at[n]))
    prefetch = [
        net.move(grads.at[above, pl.ds(0, 2)], toward),
        net.move(grads.at[below, pl.ds(2, 2)], away),
        net.move(grads.at[y], home),
    ]
    net.greet(
        [dict(y=1), dict(y=2), dict(y=3), dict(zl=1), dict(zl=2), dict(zl=3)]
        + [dict(x=1), dict(x=2), dict(x=3), dict(zh=1), dict(c=1)]
    )

    def scatter(group):
        far_up = net.push(strip(grads, beyond, 0, group), far.at[group, pl.ds(0, 2)], y=1)
        far_down = net.push(strip(grads, beyond, 2, group), far.at[group, pl.ds(2, 2)], y=3)
        near_up = net.push(strip(grads, above, 2, group), up.at[group, pl.ds(2, 2)], y=1)
        near_down = net.push(strip(grads, below, 0, group), down.at[group, pl.ds(0, 2)], y=3)
        return far_up, far_down, near_up, near_down

    def relay(group, copies):
        rows = pl.ds(group * SUB, SUB)
        copies[0].wait_recv()
        stage[group, 0:2] = far[group, 0:2] + toward[:, rows]
        first = net.push(stage.at[group, pl.ds(0, 2)], up.at[group, pl.ds(0, 2)], y=1)
        copies[1].wait_recv()
        stage[group, 2:4] = far[group, 2:4] + away[:, rows]
        second = net.push(stage.at[group, pl.ds(2, 2)], down.at[group, pl.ds(2, 2)], y=3)
        return first, second, copies[2], copies[3]

    def reduce_z(group, copies):
        for copy in copies:
            copy.wait_recv()
        mine[group] = home[:, pl.ds(group * SUB, SUB)] + up[group] + down[group]
        return [net.push(mine.at[group, (zl + k) % 4], zgot.at[group, k - 1], zl=k) for k in (1, 2, 3)]

    def turn(group, copies):
        for copy in copies:
            copy.wait_recv()
        total = mine[group, zl] + zgot[group, 0] + zgot[group, 1] + zgot[group, 2]
        for a in range(4):
            both[1, group, a] = total[:, a * 256 : (a + 1) * 256]
        kept = net.move(both.at[1, group, y], both.at[0, group, y])
        return [net.push(both.at[1, group, (y + k) % 4], both.at[0, group, y], y=k) for k in (1, 3, 2)], kept

    def gather_z(group, turned):
        copies, kept = turned
        for copy in copies:
            copy.wait_recv()
        kept.wait()
        here = chunk.at[:, zl, pl.ds(group * SUB, SUB)]
        kept = net.move(both.at[side, group], here)
        return [net.push(both.at[(zl + k) % 4 // 2, group], here, zl=k) for k in (1, 2, 3)], kept

    scattered = scatter(0)
    for copy in fetched:
        copy.wait()
    own_slot = net.move(packed.at[:, rows_of(y, 64)], slots.at[y])
    slotted = {k: net.push(packed.at[:, rows_of((y + k) % 4, 64)], slots.at[y], y=k) for k in (1, 3, 2)}
    for copy in prefetch:
        copy.wait()
    relayed = relay(0, scattered)
    scattered = scatter(1)

    spreads = []
    for k in (0, 1, 3, 2):
        if k == 0:
            own_slot.wait()
        else:
            slotted[k].wait_recv()
        at = (y + 4 - k) % 4
        for m in (0, 1, 2, 3):
            source = slots.at[at, :, rows_of((x + m) % 4, 16)]
            if m == 0:
                spreads.append(net.move(source, spread.at[x * 4 + at]))
            else:
                spreads.append(net.push(source, spread.at[x * 4 + at], x=m))
    reduced = reduce_z(0, relayed)
    relayed = relay(1, scattered)

    for n, copy in enumerate(spreads):
        if n % 4:
            copy.wait_recv()
        else:
            copy.wait()

    def chosen(n, core):
        target = (x + n % 4) % 4 * 4 + (zh + n // 4) % 2 * 2 + core
        source, slot = rank_of(owner, target)
        valid = (source // 2 % 2 == zh) & (source % 2 == c)
        values = spread[jnp.where(valid, source // 4 * 4 + slot, 0)]
        return values * jnp.where(valid, 1.0, 0.0)

    for n in range(8):
        outgo[n] = chosen(n, 1 - c)
    swapped = net.push(outgo, income, c=1)
    for n in range(8):
        near[n] = chosen(n, c)
    turned = turn(0, reduced)
    swapped.wait_recv()
    for n in range(8):
        near[n] = near[n] + income[n]
    crossing = net.push(near.at[pl.ds(4, 4)], cross, zh=1)
    reduced = reduce_z(1, relayed)
    gathered, first_kept = gather_z(0, turned)
    turned = turn(1, reduced)
    crossing.wait_recv()
    for n in range(4):
        fin[n] = near[n] + cross[n]
    place_here = oldp.at[:, rows_of(x, 16)]
    own_old = net.move(fin.at[0], place_here)
    brought = [net.push(fin.at[m], place_here, x=m) for m in (1, 2, 3)]
    more, second_kept = gather_z(1, turned)
    for copy in gathered + more:
        copy.wait_recv()
    first_kept.wait()
    second_kept.wait()

    @pl.when(side == 1)
    def _():
        for a in range(4):
            mat_high[a], mat_low[a] = split(chunk[a].reshape(256, 256).T)

    @pl.when(side == 0)
    def _():
        for a in range(4):
            mat_high[a], mat_low[a] = split(chunk[a].reshape(256, 256))

    def outer(a, b):
        return lax.dot_general(a, b, (((1,), (1,)), ((), ())), preferred_element_type=jnp.float32)

    for n in range(5):
        i = jnp.where(half == 0, PACKED[0][n][0], PACKED[1][n][0])
        j = jnp.where(half == 0, PACKED[0][n][1], PACKED[1][n][1])
        left_high, right_high = mat_high[i], mat_high[j]
        gram[n] = (
            outer(left_high, mat_low[j]) + outer(mat_low[i], right_high) + outer(left_high, right_high)
        )
    summed = [net.push(gram.at[:, rows_of((y + k) % 4, 64)], ggot.at[k - 1], y=k) for k in (1, 3, 2)]
    own_old.wait()
    for copy in brought + summed:
        copy.wait_recv()
    piece[...] = 0.6 * oldp[...] + (1.0 - 0.6) * (gram[:, rows_of(y, 64)] + ggot[0] + ggot[1] + ggot[2])

    here = columns.at[x * 2 + zh]
    there = sall.at[half, :, y]
    own = net.move(piece, here)
    own_piece = net.move(piece, there)
    across = net.push(piece, here, zh=1)
    first_up = net.push(piece, here, x=1)
    first_down = net.push(piece, here, x=3)
    halved = net.push(piece, there, half=1)
    y_up = net.push(piece, there, y=1)
    y_down = net.push(piece, there, y=3)
    back, on = (x + 3) % 4, (x + 1) % 4
    first_up.wait_recv()
    there = columns.at[back * 2 + zh]
    first_far = net.push(there, there, x=1)
    y_up.wait_recv()
    there = sall.at[half, :, below]
    y_far = net.push(there, there, y=1)
    halved.wait_recv()
    there = sall.at[1 - half, :, y]
    other_down = net.push(there, there, y=3)
    other_up = net.push(there, there, y=1)
    across.wait_recv()
    there = columns.at[x * 2 + 1 - zh]
    second_down = net.push(there, there, x=3)
    second_up = net.push(there, there, x=1)
    other_down.wait_recv()
    there = sall.at[1 - half, :, above]
    other_far = net.push(there, there, y=3)
    second_down.wait_recv()
    there = columns.at[on * 2 + 1 - zh]
    second_far = net.push(there, there, x=3)
    own.wait()
    for copy in (first_down, first_far, second_up, second_far):
        copy.wait_recv()

    def wanted(k, core):
        found, source = block_at(owner, x * 4 + zh * 2 + core, (y + k) % 4)
        valid = (found == 1) & (source % 2 == c)
        return columns[jnp.where(valid, source // 2, 0)] * jnp.where(valid, 1.0, 0.0)

    swapped = {}
    for k in (2, 1, 3, 0):
        leave[k] = wanted(k, 1 - c)
        swapped[k] = net.push(leave.at[k], enter.at[k], c=1)
    sent = {}
    for k in (2, 1, 3, 0):
        ready[k] = wanted(k, c)
        swapped[k].wait_recv()
        ready[k] = ready[k] + enter[k]
        if k:
            sent[k] = net.push(ready.at[k], parts.at[:, y], y=k)
        else:
            own = net.move(ready.at[0], parts.at[:, y])

    own_piece.wait()
    for copy in (y_down, y_far, other_up, other_far):
        copy.wait_recv()
    for h in range(2):
        for n in range(5):
            i, j = PACKED[h][n]
            stat[pl.ds(i * 256, 256), pl.ds(j * 256, 256)] = sall[h, n].reshape(256, 256)
    for i, j in ((0, 1), (0, 2), (0, 3), (2, 1), (3, 1), (2, 3)):
        stat[pl.ds(j * 256, 256), pl.ds(i * 256, 256)] = stat[pl.ds(i * 256, 256), pl.ds(j * 256, 256)].T
    find_root((y, zl), stat, rootbuf, column, base, high, low)
    returned = net.push(rootbuf.at[1], roots.at[side], side=1)
    kept = net.move(rootbuf.at[0], roots.at[side])

    own.wait()
    halves = []
    for k in (0, 1, 3, 2):
        if k:
            sent[k].wait_recv()
        at = (y + 4 - k) % 4
        halves.append(net.push(parts.at[pl.ds(3, 2), at], crossed.at[:, at], half=1))
    for copy in halves:
        copy.wait_recv()
    kept.wait()
    returned.wait_recv()
    net.close()


def finish_kernel(spot, packed, crossed, old, new):
    half, present = spot[0], spot[1]

    @pl.when(present == 0)
    def _():
        new[...] = 0.6 * old[...]

    @pl.when(present != 0)
    def _():
        def put(i, j, values):
            new[pl.ds(i * 256, 256), pl.ds(j * 256, 256)] = values

        @pl.when(half == 0)
        def _():
            put(0, 0, packed[0])
            put(0, 1, packed[1])
            put(0, 2, packed[3])
            put(0, 3, packed[4])
            put(1, 0, packed[1].T)
            put(1, 1, packed[2])
            put(1, 2, crossed[0].T)
            put(1, 3, crossed[1].T)

        @pl.when(half == 1)
        def _():
            put(0, 0, crossed[0].T)
            put(0, 1, packed[3])
            put(0, 2, packed[0])
            put(0, 3, packed[1])
            put(1, 0, crossed[1].T)
            put(1, 1, packed[4])
            put(1, 2, packed[1].T)
            put(1, 3, packed[2])


def local_call(kernel, out_shape, operands, scratch, flops, traffic):
    return pl.pallas_call(
        kernel,
        out_shape=out_shape,
        in_specs=[pl.BlockSpec(memory_space=pltpu.SMEM)]
        + [pl.BlockSpec(memory_space=pltpu.VMEM)] * (len(operands) - 1),
        out_specs=jax.tree.map(lambda _: pl.BlockSpec(memory_space=pltpu.VMEM), out_shape),
        scratch_shapes=scratch,
        cost_estimate=pl.CostEstimate(flops=flops, bytes_accessed=traffic, transcendentals=0),
        compiler_params=pltpu.CompilerParams(vmem_limit_bytes=VMEM_LIMIT),
    )(*operands)


def f32(*shape):
    return jax.ShapeDtypeStruct(shape, jnp.float32)


def refresh(owner, grads, old):
    strips = (GROUPS, 4, SUB, BS)
    piece = (5, 64, 256)
    scratch = [strips, strips, strips, (2, 64, BS), (2, 64, BS), (4, 64, BS), strips, strips, (GROUPS, 3, SUB, BS)]
    scratch += [(5, 256, 256), (4, *piece), (16, 5, 16, 256), (8, 5, 16, 256), (8, 5, 16, 256), (8, 5, 16, 256)]
    scratch += [(4, 5, 16, 256), (4, 5, 16, 256), piece]
    scratch += [(2, GROUPS, 4, SUB, 256), (4, 4, 64, 256), (5, 256, 256), (3, *piece), (2, 5, 4, 64, 256)]
    scratch += [(BS, BS), (BS, 1), (BS, BS), (2, 64, BS)]
    scratch += [(8, *piece), (4, *piece), (4, *piece), (4, *piece), piece]
    halves = [(4, 256, 256), (4, 256, 256), (BS, BS), (BS, BS)]
    out_shape = (f32(5, 4, 64, 256), f32(2, 4, 64, 256), f32(2, 64, BS))
    return pl.pallas_call(
        refresh_kernel,
        out_shape=out_shape,
        in_specs=[pl.BlockSpec(memory_space=pltpu.SMEM)] + [pl.BlockSpec(memory_space=pl.ANY)] * 2,
        out_specs=tuple(pl.BlockSpec(memory_space=pl.ANY) for _ in out_shape),
        scratch_shapes=[pltpu.VMEM(shape, jnp.float32) for shape in scratch]
        + [pltpu.VMEM(shape, jnp.bfloat16) for shape in halves]
        + [
            pltpu.SemaphoreType.DMA((80,)),
            pltpu.SemaphoreType.DMA((80,)),
            pltpu.SemaphoreType.DMA((24,)),
        ],
        compiler_params=pltpu.CompilerParams(
            collective_id=0, has_side_effects=True, vmem_limit_bytes=VMEM_LIMIT
        ),
    )(owner, grads, old)


def per_device(grads, owner, stats):
    block = lax.axis_index("block")
    y, zl, *_ = place(lax.axis_index("dp"), block)
    old = stats[0, 0]
    parts, crossed, roots = refresh(owner, grads.reshape(4, 4, 64, BS), old)
    present = jnp.sum((owner == block).astype(jnp.int32)) > y
    new = local_call(
        finish_kernel,
        f32(512, BS),
        [
            jnp.stack([zl % 2, present.astype(jnp.int32)]).astype(jnp.int32),
            parts.reshape(5, 256, 256),
            crossed.reshape(2, 256, 256),
            old,
        ],
        [],
        2**20,
        6 * 2**20,
    )
    return new[None, None], roots[None]


def solution(mesh):
    return jax.shard_map(
        per_device,
        mesh=mesh,
        in_specs=(P("dp", "block", None, None), P(), P("block", "dp", None, None)),
        out_specs=(P("block", "dp", None, None), P("block", None, "dp", None)),
        check_vma=False,
    )
```

time: 776 us -> 207 us (0.27)
  waiting for transfers between devices: 604 us -> 0 us
  Pallas kernels: 0 us -> 201 us
  matrix products: 83.5 us -> 0 us
  other arithmetic: 28.3 us -> 1.87 us
  between operations: 20.8 us -> 1.34 us
  local copies, waits for them, and re-layouts: 17.9 us -> 0.8 us
  starting transfers between devices: 11.7 us -> 0 us
    reduce_scatter x2 -> x0, waiting for transfers between devices: 247 us -> none  [the longest x1 138 us: per_device(): lax.psum_scatter(outgoing_blocks, 'block', scatter_dimension=0, tiled=True)]
    pallas_call x0 -> x2, Pallas kernels: none -> 201 us  [the longest x1 197 us: refresh(): pl.pallas_call(refresh_kernel, out_shape=out_shape, in_specs=[pl.BlockSpe...]
    all_to_all x2 -> x0, waiting for transfers between devices: 145 us -> none  [the longest x1 97.2 us: per_device(): lax.all_to_all(outgoing, 'dp', split_axis=0, concat_axis=0, tiled=True)]
    ppermute x3 -> x0, waiting for transfers between devices: 136 us -> none  [swapped(): lax.ppermute(array, axis, [(i, i ^ 1 << distance) for i in range(lax.axis...]
    dot_general x14 -> x0, matrix products: 83.5 us -> none  [the longest x13 76.4 us: product(): return jnp.dot(left_side, right_side, precision=lax.Precision.HIGHEST)]
    all_gather x1 -> x0, waiting for transfers between devices: 74.6 us -> none  [per_device(): everywhere = lax.all_gather(reduced, 'block', axis=0, tiled=True)]
    select_n x6 -> x0, other arithmetic: 11.2 us -> none  [the longest x1 4.53 us: per_device(): oriented = jnp.where(stat_kind == 0, gradient, gradient.T)]
    all_to_all x2 -> x0, starting transfers between devices: 10.1 us -> none  [the longest x1 5.58 us: per_device(): lax.all_to_all(root_columns.reshape(dp_count, slab_rows, half_order), 'dp...]
  transfers between devices with their start and end apart: 8 -> 0, of which waited for: 8 -> 0; matrix products, arithmetic and copies ran while one was open for 0% -> 0% of each run, Pallas kernels for 0% -> 0%
where the time goes in v1:
time: 207 us; the launch traced here: 205 us
  Pallas kernels  201 us (97%)
    pallas_call x1, Pallas kernels, refresh(): pl.pallas_call(refresh_kernel, out_shape=out_shape, in_specs=[pl.BlockSpe...  197 us

profile of v1, /device:TPU:4, one launch (start us, length us, event | category | flops | bytes accessed | tf_op | source)
XLA Modules:
  0.0 204.5 jit_solution(17600721280007505856)
XLA Ops:
  0.7 1.3 fusion
  2.6 0.6 pad_add_fusion.spot
  3.2 196.7 %shard_map.50 = (f32[5,4,64,256]{3,2,1,0:T(8,128)}, f32[2,4,64,256]{3,2,1,0:T(8,128)}, f32[2,64,1024]{2,1,0:T(8,128)}) custom-call(s32[16]{0:T(128)} %owner.1, f32[4,4,64,1024]{3,2,1,0:T(8,128)} %bitcast.10, f32[512,1024]{1,0:T(8,128)} %bitcast.8), custom_call_target="tpu_custom_call" | custom-call | tf_op jit(solution)/shard_map/pallas_call | solution.py:469
  199.9 0.0 copy-start
  199.9 3.8 %shard_map.51 = f32[512,1024]{1,0:T(8,128)} custom-call(s32[2]{0:T(128)} %pad_add_fusion.spot, f32[5,256,256]{2,1,0:T(8,128)} %bitcast.12, f32[2,256,256]{2,1,0:T(8,128)} %bitcast.13, f32[512,1024]{1,0:T(8,128)} %bitcast.9), custom_call_target="tpu_custom_call" | custom-call | flops 1048576 | bytes 6291456 | tf_op jit(solution)/shard_map/pallas_call | solution.py:442
  203.7 0.0 copy-done
  203.7 0.8 copy.6
Async XLA Ops:
  199.9 3.9 %copy-start = (f32[2,64,1024]{2,1,0:T(8,128)S(1)}, f32[2,64,1024]{2,1,0:T(8,128)}, u32[]{:S(2)}) copy-start(f32[2,64,1024]{2,1,0:T(8,128)} %get-tuple-element.7) | copy-start | bytes 1572868

commit v2 on v1

v2 whole, which is shorter than its diff:
```python
import jax
import jax.numpy as jnp
from jax import lax
from jax.experimental import pallas as pl
from jax.experimental.pallas import tpu as pltpu
from jax.sharding import PartitionSpec as P

PSTEPS = 8
BS = 1024
GROUPS = 4
SUB = 64 // GROUPS
MESH = pl.DeviceIdType.MESH
VMEM_LIMIT = 60 * 1024 * 1024

PACKED = (
    ((0, 2), (0, 3), (0, 0), (0, 1), (1, 1)),
    ((2, 1), (3, 1), (2, 2), (2, 3), (3, 3)),
)
SETS = (pl.ds(0, 2), pl.ds(2, 3))


GRADS, OLD = 0, 1
ORDER = (
    (GRADS, 1, 0), (GRADS, 0, 2), (OLD, 2, 0), (GRADS, 1, 1), (GRADS, 2, 0), (OLD, 1, 1), (GRADS, 0, 3),
    (GRADS, 1, 2), (GRADS, 3, 0), (GRADS, 2, 1), (GRADS, 4, 0), (OLD, 3, 0), (GRADS, 1, 3), (GRADS, 3, 1),
    (GRADS, 2, 2), (GRADS, 5, 0), (GRADS, 4, 1), (OLD, 4, 0), (OLD, 2, 1), (GRADS, 2, 3), (GRADS, 3, 2),
    (GRADS, 6, 0), (GRADS, 5, 1), (GRADS, 4, 2), (OLD, 5, 0), (OLD, 3, 1), (GRADS, 3, 3), (GRADS, 6, 1),
    (GRADS, 5, 2), (GRADS, 4, 3), (OLD, 4, 1), (GRADS, 6, 2), (GRADS, 5, 3), (GRADS, 6, 3), (OLD, 5, 1),
)


def place(dp, block):
    return dp // 4, dp % 4, block // 4, block // 2 % 2, block % 2


class Network:
    def __init__(self, send, recv, local):
        self.send, self.recv, self.local = send, recv, local
        self.count = self.locals = 0
        self.sent = []
        self.dp, self.block = lax.axis_index("dp"), lax.axis_index("block")
        self.y, self.zl, self.x, self.zh, self.c = place(self.dp, self.block)

    def device(self, y=0, zl=0, x=0, zh=0, c=0, half=0, side=0):
        row = (self.zl + zl) % 4
        if half:
            row = row + 1 - 2 * (row % 2)
        if side:
            row = (row + 2) % 4
        return (
            (self.y + y) % 4 * 4 + row,
            (self.x + x) % 4 * 4 + (self.zh + zh) % 2 * 2 + (self.c + c) % 2,
        )

    def greet(self, steps):
        barrier = pltpu.get_barrier_semaphore()
        for step in steps:
            pl.semaphore_signal(barrier, inc=1, device_id=self.device(**step), device_id_type=MESH)
        pl.semaphore_wait(barrier, len(steps))

    def push(self, source, target, **step):
        n = self.count
        self.count += 1
        copy = pltpu.make_async_remote_copy(
            src_ref=source,
            dst_ref=target,
            send_sem=self.send.at[n],
            recv_sem=self.recv.at[n],
            device_id=self.device(**step),
            device_id_type=MESH,
        )
        copy.start()
        self.sent.append(copy)
        return copy

    def move(self, source, target):
        copy = pltpu.make_async_copy(source, target, self.local.at[self.locals])
        self.locals += 1
        copy.start()
        return copy

    def close(self):
        for copy in self.sent:
            copy.wait_send()


def split(values):
    high = values.astype(jnp.bfloat16)
    return high, (values - high.astype(jnp.float32)).astype(jnp.bfloat16)


def rank_of(owner, block):
    mine = owner[block]
    count = lax.fori_loop(
        0, 16, lambda i, n: n + jnp.where((i < block) & (owner[i] == mine), 1, 0), jnp.int32(0)
    )
    return mine, count


def block_at(owner, column, wanted):
    def step(i, carry):
        count, found, source = carry
        hit = owner[i] == column
        here = hit & (count == wanted)
        return count + jnp.where(hit, 1, 0), jnp.where(here, 1, found), jnp.where(here, i, source)

    zero = jnp.int32(0)
    _, found, source = lax.fori_loop(0, 16, step, (zero, zero, zero))
    return found, source


def top_value(stat, column):

    def to_column(row):
        @pl.loop(0, 8)
        def _(i):
            rows = pl.ds(pl.multiple_of(i * 128, 128), 128)
            column[rows, :] = jnp.sum(stat[rows, :] * row, axis=1, keepdims=True)

        return column[...]

    def to_row(values):
        column[...] = values

        def body(i, total):
            rows = pl.ds(pl.multiple_of(i * 128, 128), 128)
            return total + jnp.sum(stat[rows, :] * column[rows, :], axis=0, keepdims=True)

        return lax.fori_loop(0, 8, body, jnp.zeros((1, BS), jnp.float32))

    row = jnp.full((1, BS), BS ** (-0.5), jnp.float32)
    for _ in range(PSTEPS // 2):
        image = to_column(row)
        image = image / jnp.sqrt(jnp.sum(image * image))
        row = to_row(image)
        row = row / jnp.sqrt(jnp.sum(row * row))
    image = to_column(row)
    return jnp.sqrt(jnp.sum(image * image, axis=(0, 1), keepdims=True))


def find_root(spot, top, stat, root, base, high, low):
    y, zl = spot
    scale = 2.5 / top
    fourth = jnp.sqrt(jnp.sqrt(scale))

    @pl.loop(0, 4)
    def _(i):
        rows = pl.ds(pl.multiple_of(i * 256, 256), 256)
        eye = lax.broadcasted_iota(jnp.int32, (256, BS), 0) + i * 256 == lax.broadcasted_iota(
            jnp.int32, (256, BS), 1
        )
        values = (jnp.where(eye, 5.0, 0.0) - scale * stat[rows, :]) / 4.0
        base[rows, :] = values
        upper, lower = split(values)
        high[rows, :] = upper
        low[rows, :] = lower

    def times(left):
        upper, lower = split(left)

        def product(a, b):
            return jnp.dot(a, b, preferred_element_type=jnp.float32)

        both = product(jnp.concatenate([upper, lower], axis=0), high[...])
        return both[128:] + product(upper, low[...]) + both[:128]

    own = pl.multiple_of((y * 4 + zl) * 64, 64)
    other = pl.multiple_of((y * 4 + (zl + 2) % 4) * 64, 64)
    first = jnp.concatenate([base[pl.ds(own, 64), :], base[pl.ds(other, 64), :]], axis=0)
    power = times(times(times(first)))
    result = (5.0 * first + times(4.0 * times(power) - 5.0 * power)) * (fourth / 4.0)
    root[0] = result[:64]
    root[1] = result[64:]


def refresh_kernel(owner, grads, old, new_out, roots, *scratch):
    far, up, down, stage, mine, middle, first_got, second_got, toward, away, home = scratch[:11]
    packed, slots, oldp, both, chunk, gram, ggot, sall, stat, column, base, rootbuf = scratch[11:23]
    piece, parts, crossed, new = scratch[23:27]
    spread, outgo, income, near, cross, fin = (scratch[27 + 2 * n : 29 + 2 * n] for n in range(6))
    columns, leave, enter, ready = (scratch[39 + 2 * n : 41 + 2 * n] for n in range(4))
    mat_high, mat_low, high, low = scratch[47:51]
    net = Network(*scratch[51:])
    y, zl, x, zh, c = net.y, net.zl, net.x, net.zh, net.c
    side, half = zl // 2, zl % 2
    below, above, beyond = (y + 3) % 4, (y + 1) % 4, (y + 2) % 4

    def rows_of(at, size):
        return pl.ds(pl.multiple_of(at * size, size), size)

    def strip(ref, chunk_at, first, group):
        return ref.at[chunk_at, pl.ds(first, 2), pl.ds(group * SUB, SUB)]

    fetched = []
    for n in range(5):
        i = jnp.where(half == 0, PACKED[0][n][0], PACKED[1][n][0] - 2)
        j = jnp.where(half == 0, PACKED[0][n][1], PACKED[1][n][1])
        fetched.append(net.move(old.at[rows_of(i, 256), rows_of(j, 256)], packed.at[n]))
    prefetch = [
        net.move(grads.at[above, pl.ds(0, 2)], toward),
        net.move(grads.at[below, pl.ds(2, 2)], away),
        net.move(grads.at[y], home),
    ]
    kept_old = net.move(old, new)
    net.greet(
        [dict(y=1), dict(y=2), dict(y=3), dict(half=1), dict(side=1)]
        + [dict(x=1), dict(x=2), dict(x=3), dict(zh=1), dict(c=1)]
    )

    def scatter(group):
        far_up = net.push(strip(grads, beyond, 0, group), far.at[group, pl.ds(0, 2)], y=1)
        far_down = net.push(strip(grads, beyond, 2, group), far.at[group, pl.ds(2, 2)], y=3)
        near_up = net.push(strip(grads, above, 2, group), up.at[group, pl.ds(2, 2)], y=1)
        near_down = net.push(strip(grads, below, 0, group), down.at[group, pl.ds(0, 2)], y=3)
        return far_up, far_down, near_up, near_down

    def relay(group, copies):
        rows = pl.ds(group * SUB, SUB)
        copies[0].wait_recv()
        stage[group, 0:2] = far[group, 0:2] + toward[:, rows]
        first = net.push(stage.at[group, pl.ds(0, 2)], up.at[group, pl.ds(0, 2)], y=1)
        copies[1].wait_recv()
        stage[group, 2:4] = far[group, 2:4] + away[:, rows]
        second = net.push(stage.at[group, pl.ds(2, 2)], down.at[group, pl.ds(2, 2)], y=3)
        return first, second, copies[2], copies[3]

    def reduce_half(group, copies):
        for copy in copies:
            copy.wait_recv()
        for n in range(4):
            mine[group, n % 2, n // 2] = home[n, pl.ds(group * SUB, SUB)] + up[group, n] + down[group, n]
        return net.push(mine.at[group, 1 - half], first_got.at[group], half=1)

    def reduce_side(group, copy):
        copy.wait_recv()
        middle[group] = mine[group, half] + first_got[group]
        return net.push(middle.at[group, 1 - side], second_got.at[group], side=1)

    def turn(group, copy):
        copy.wait_recv()
        total = middle[group, side] + second_got[group]
        for a in range(4):
            both[1, group, a] = total[:, a * 256 : (a + 1) * 256]
        kept = net.move(both.at[1, group, y], both.at[0, group, y])
        return [net.push(both.at[1, group, (y + k) % 4], both.at[0, group, y], y=k) for k in (1, 3, 2)], kept

    def rows_in(device, group):
        return chunk.at[:, device, pl.ds(group * SUB, SUB)]

    def gather_side(group, turned):
        copies, kept = turned
        for copy in copies:
            copy.wait_recv()
        kept.wait()
        here = rows_in(zl, group)
        from_side = net.push(both.at[1 - side, group], here, side=1)
        from_half = net.push(both.at[side, group], here, half=1)
        return from_side, from_half, net.move(both.at[side, group], here)

    def gather_half(group, copies):
        copies[0].wait_recv()
        there = rows_in((zl + 2) % 4, group)
        return net.push(there, there, half=1), copies[1], copies[2]

    def start_old(n):
        part = SETS[n]
        own = net.move(packed.at[part, rows_of(y, 64)], slots.at[y, part])
        return own, {
            k: net.push(packed.at[part, rows_of((y + k) % 4, 64)], slots.at[y, part], y=k) for k in (1, 3, 2)
        }

    def spread_old(n, started):
        own, slotted = started
        local, remote = [], []
        for k in (0, 1, 3, 2):
            if k == 0:
                own.wait()
            else:
                slotted[k].wait_recv()
            at = (y + 4 - k) % 4
            for m in (0, 1, 2, 3):
                source = slots.at[at, SETS[n], rows_of((x + m) % 4, 16)]
                if m == 0:
                    local.append(net.move(source, spread[n].at[x * 4 + at]))
                else:
                    remote.append(net.push(source, spread[n].at[x * 4 + at], x=m))
        return local, remote

    def swap_old(n, spreads):
        for copy in spreads[0]:
            copy.wait()
        for copy in spreads[1]:
            copy.wait_recv()
        for i, (index, mask) in enumerate(old_away):
            outgo[n][i] = spread[n][index] * mask
        return net.push(outgo[n], income[n], c=1)

    def cross_old(n, swapped):
        for i, (index, mask) in enumerate(old_home):
            near[n][i] = spread[n][index] * mask
        swapped.wait_recv()
        for i in range(8):
            near[n][i] = near[n][i] + income[n][i]
        return net.push(near[n].at[pl.ds(4, 4)], cross[n], zh=1)

    def finish_old(n, crossing):
        crossing.wait_recv()
        for i in range(4):
            fin[n][i] = near[n][i] + cross[n][i]
        here = oldp.at[SETS[n], rows_of(x, 16)]
        own = net.move(fin[n].at[0], here)
        return own, [net.push(fin[n].at[m], here, x=m) for m in (1, 2, 3)]

    def lookup_old(n, core):
        target = (x + n % 4) % 4 * 4 + (zh + n // 4) % 2 * 2 + core
        source, slot = rank_of(owner, target)
        valid = (source // 2 % 2 == zh) & (source % 2 == c)
        return jnp.where(valid, source // 4 * 4 + slot, 0), jnp.where(valid, 1.0, 0.0)

    def lookup_slot(k, core):
        found, source = block_at(owner, x * 4 + zh * 2 + core, (y + k) % 4)
        valid = (found == 1) & (source % 2 == c)
        return jnp.where(valid, source // 2, 0), jnp.where(valid, 1.0, 0.0)

    stages = (scatter, relay, reduce_half, reduce_side, turn, gather_side, gather_half)
    steps = (None, start_old, spread_old, swap_old, cross_old, finish_old)
    state, olds = {}, {}

    def run(stage, group):
        if stage == 0:
            state[group] = scatter(group)
        else:
            state[group] = stages[stage](group, state[group])

    def run_old(step, n):
        if step == 1:
            olds[n] = start_old(n)
        else:
            olds[n] = steps[step](n, olds[n])

    run(0, 0)
    for copy in fetched:
        copy.wait()
    run_old(1, 0)
    run(0, 1)
    old_away = [lookup_old(n, 1 - c) for n in range(8)]
    old_home = [lookup_old(n, c) for n in range(8)]
    for copy in prefetch:
        copy.wait()
    for job in ORDER:
        if job[0] == GRADS:
            run(job[1], job[2])
        else:
            run_old(job[1], job[2])
    kept_old.wait()
    members = lax.fori_loop(0, 16, lambda i, n: n + jnp.where(owner[i] == net.block, 1, 0), jnp.int32(0))
    new[...] = new[...] * jnp.where(members > y, 0.0, 0.6)
    slot_away = [lookup_slot(k, 1 - c) for k in range(4)]
    slot_home = [lookup_slot(k, c) for k in range(4)]
    for relayed, direct, kept in state.values():
        relayed.wait_recv()
        direct.wait_recv()
        kept.wait()

    @pl.when(side == 1)
    def _():
        for a in range(4):
            mat_high[a], mat_low[a] = split(chunk[a].reshape(256, 256).T)

    @pl.when(side == 0)
    def _():
        for a in range(4):
            mat_high[a], mat_low[a] = split(chunk[a].reshape(256, 256))

    def outer(a, b):
        return lax.dot_general(a, b, (((1,), (1,)), ((), ())), preferred_element_type=jnp.float32)

    summed = []
    for part in SETS:
        for n in range(part.start, part.start + part.size):
            i = jnp.where(half == 0, PACKED[0][n][0], PACKED[1][n][0])
            j = jnp.where(half == 0, PACKED[0][n][1], PACKED[1][n][1])
            left_high, right_high = mat_high[i], mat_high[j]
            gram[n] = (
                outer(left_high, mat_low[j]) + outer(mat_low[i], right_high) + outer(left_high, right_high)
            )
        summed.append(
            [
                net.push(gram.at[part, rows_of((y + k) % 4, 64)], ggot.at[k - 1, part], y=k)
                for k in (1, 3, 2)
            ]
        )
    back, on = (x + 3) % 4, (x + 1) % 4
    own, across, first_up, first_down = [], [], [], []
    halved, y_up, y_down, y_far, other_up, other_down, other_far, own_piece = [], [], [], [], [], [], [], []
    for n, part in enumerate(SETS):
        olds[n][0].wait()
        for copy in olds[n][1]:
            copy.wait_recv()
        for copy in summed[n]:
            copy.wait_recv()
        piece[part] = 0.6 * oldp[part] + (1.0 - 0.6) * (
            gram[part, rows_of(y, 64)] + ggot[0, part] + ggot[1, part] + ggot[2, part]
        )
        here, there = columns[n].at[x * 2 + zh], sall.at[half, part, y]
        halved.append(net.push(piece.at[part], there, half=1))
        across.append(net.push(piece.at[part], here, zh=1))
        first_up.append(net.push(piece.at[part], here, x=1))
        first_down.append(net.push(piece.at[part], here, x=3))
        y_up.append(net.push(piece.at[part], there, y=1))
        y_down.append(net.push(piece.at[part], there, y=3))
        own.append(net.move(piece.at[part], here))
        own_piece.append(net.move(piece.at[part], there))

    first_far, second_up, second_down, second_far = [], [], [], []

    def pass_first(n):
        first_up[n].wait_recv()
        there = columns[n].at[back * 2 + zh]
        first_far.append(net.push(there, there, x=1))

    def start_second(n):
        across[n].wait_recv()
        there = columns[n].at[x * 2 + 1 - zh]
        second_down.append(net.push(there, there, x=3))
        second_up.append(net.push(there, there, x=1))

    def pass_second(n):
        second_down[n].wait_recv()
        there = columns[n].at[on * 2 + 1 - zh]
        second_far.append(net.push(there, there, x=3))

    def choose(n):
        own[n].wait()
        for copy in (first_down[n], first_far[n], second_up[n], second_far[n]):
            copy.wait_recv()
        swapped = {}
        for k in (2, 1, 3, 0):
            index, mask = slot_away[k]
            leave[n][k] = columns[n][index] * mask
            swapped[k] = net.push(leave[n].at[k], enter[n].at[k], c=1)
        sent = {}
        for k in (2, 1, 3, 0):
            index, mask = slot_home[k]
            ready[n][k] = columns[n][index] * mask
            swapped[k].wait_recv()
            ready[n][k] = ready[n][k] + enter[n][k]
            here = parts.at[SETS[n], y]
            if k:
                sent[k] = net.push(ready[n].at[k], here, y=k)
            else:
                kept = net.move(ready[n].at[0], here)
        return sent, kept

    def pass_own(n):
        y_up[n].wait_recv()
        there = sall.at[half, SETS[n], below]
        y_far.append(net.push(there, there, y=1))

    def start_other(n):
        halved[n].wait_recv()
        there = sall.at[1 - half, SETS[n], y]
        other_down.append(net.push(there, there, y=3))
        other_up.append(net.push(there, there, y=1))

    def pass_other(n):
        other_down[n].wait_recv()
        there = sall.at[1 - half, SETS[n], above]
        other_far.append(net.push(there, there, y=3))

    pass_first(0)
    pass_own(0)
    start_other(0)
    start_second(0)
    pass_first(1)
    pass_own(1)
    start_other(1)
    pass_second(0)
    pass_other(0)
    start_second(1)
    pass_other(1)
    sent = [choose(0)]
    pass_second(1)

    for n in range(2):
        own_piece[n].wait()
        for copy in (y_down[n], y_far[n], other_up[n], other_far[n]):
            copy.wait_recv()
    for h in range(2):
        for n in range(5):
            i, j = PACKED[h][n]
            stat[pl.ds(i * 256, 256), pl.ds(j * 256, 256)] = sall[h, n].reshape(256, 256)
    for i, j in ((0, 1), (0, 2), (0, 3), (2, 1), (3, 1), (2, 3)):
        stat[pl.ds(j * 256, 256), pl.ds(i * 256, 256)] = stat[pl.ds(i * 256, 256), pl.ds(j * 256, 256)].T
    top = top_value(stat, column)
    sent.append(choose(1))

    halves = []
    for k in (0, 1, 3, 2):
        if k:
            sent[0][0][k].wait_recv()
        else:
            sent[0][1].wait()
        at = (y + 4 - k) % 4
        halves.append(net.push(parts.at[SETS[0], at], crossed.at[:, at], half=1))
    find_root((y, zl), top, stat, rootbuf, base, high, low)
    returned = net.push(rootbuf.at[1], roots.at[side], side=1)
    kept = net.move(rootbuf.at[0], roots.at[side])

    sent[1][1].wait()
    for k in (1, 3, 2):
        sent[1][0][k].wait_recv()
    for copy in halves:
        copy.wait_recv()

    def put(i, j, values):
        rows, cols = pl.ds(i * 256, 256), pl.ds(j * 256, 256)
        new[rows, cols] = new[rows, cols] + values

    def part(n):
        return parts[n].reshape(256, 256)

    def turned_part(n):
        return crossed[n].reshape(256, 256).T

    @pl.when(half == 0)
    def _():
        put(0, 0, part(2))
        put(0, 1, part(3))
        put(0, 2, part(0))
        put(0, 3, part(1))
        put(1, 0, part(3).T)
        put(1, 1, part(4))
        put(1, 2, turned_part(0))
        put(1, 3, turned_part(1))

    @pl.when(half == 1)
    def _():
        put(0, 0, turned_part(0))
        put(0, 1, part(0))
        put(0, 2, part(2))
        put(0, 3, part(3))
        put(1, 0, turned_part(1))
        put(1, 1, part(1))
        put(1, 2, part(3).T)
        put(1, 3, part(4))

    written = net.move(new, new_out)
    kept.wait()
    returned.wait_recv()
    written.wait()
    net.close()


def f32(*shape):
    return jax.ShapeDtypeStruct(shape, jnp.float32)


def refresh(owner, grads, old):
    strips, rows = (GROUPS, 4, SUB, BS), (GROUPS, 2, SUB, BS)
    piece = (5, 64, 256)
    scratch = [strips, strips, strips, strips, (GROUPS, 2, 2, SUB, BS), rows, rows, (GROUPS, SUB, BS)]
    scratch += [(2, 64, BS), (2, 64, BS), (4, 64, BS), (5, 256, 256), (4, *piece), piece]
    scratch += [(2, GROUPS, 4, SUB, 256), (4, 4, 64, 256), (5, 256, 256), (3, *piece), (2, 5, 4, 64, 256)]
    scratch += [(BS, BS), (BS, 1), (BS, BS), (2, 64, BS)]
    scratch += [piece, (5, 4, 64, 256), (2, 4, 64, 256), (512, BS)]
    for count, rows in ((16, 16), (8, 16), (8, 16), (8, 16), (4, 16), (4, 16), (8, 64), (4, 64), (4, 64), (4, 64)):
        scratch += [(count, part.size, rows, 256) for part in SETS]
    halves = [(4, 256, 256), (4, 256, 256), (BS, BS), (BS, BS)]
    out_shape = (f32(512, BS), f32(2, 64, BS))
    return pl.pallas_call(
        refresh_kernel,
        out_shape=out_shape,
        in_specs=[pl.BlockSpec(memory_space=pltpu.SMEM)] + [pl.BlockSpec(memory_space=pl.ANY)] * 2,
        out_specs=tuple(pl.BlockSpec(memory_space=pl.ANY) for _ in out_shape),
        scratch_shapes=[pltpu.VMEM(shape, jnp.float32) for shape in scratch]
        + [pltpu.VMEM(shape, jnp.bfloat16) for shape in halves]
        + [
            pltpu.SemaphoreType.DMA((160,)),
            pltpu.SemaphoreType.DMA((160,)),
            pltpu.SemaphoreType.DMA((48,)),
        ],
        compiler_params=pltpu.CompilerParams(
            collective_id=0, has_side_effects=True, vmem_limit_bytes=VMEM_LIMIT
        ),
    )(owner, grads, old)


def per_device(grads, owner, stats):
    new, roots = refresh(owner, grads.reshape(4, 4, 64, BS), stats[0, 0])
    return new[None, None], roots[None]


def solution(mesh):
    return jax.shard_map(
        per_device,
        mesh=mesh,
        in_specs=(P("dp", "block", None, None), P(), P("block", "dp", None, None)),
        out_specs=(P("block", "dp", None, None), P("block", None, "dp", None)),
        check_vma=False,
    )
```

time: 207 us -> 178 us (0.86)
  Pallas kernels: 201 us -> 170 us
  local copies, waits for them, and re-layouts: 0.8 us -> 4.01 us
    pallas_call x1, Pallas kernels: 197 us -> 170 us  [refresh(): pl.pallas_call(refresh_kernel, out_shape=out_shape, in_specs=[pl.BlockSpe...]
    pallas_call x1 -> x0, Pallas kernels: 3.85 us -> none  [local_call(): pl.pallas_call(kernel, out_shape=out_shape, in_specs=[pl.BlockSpec(memory...]
    unnamed x3 -> x4, local copies, waits for them, and re-layouts: 0.8 us -> 4.01 us
where the time goes in v2:
time: 178 us; the launch traced here: 174 us
  Pallas kernels  170 us (96%)
  local copies, waits for them, and re-layouts  4.01 us (2%)
    pallas_call x1, Pallas kernels, refresh(): pl.pallas_call(refresh_kernel, out_shape=out_shape, in_specs=[pl.BlockSpe...  170 us
    unnamed x4, local copies, waits for them, and re-layouts  4.01 us

profile of v2, /device:TPU:4, one launch (start us, length us, event | category | flops | bytes accessed | tf_op | source)
XLA Modules:
  0.0 174.2 jit_solution(1222895766753201685)
XLA Ops:
  0.6 169.6 %shard_map.50 = (f32[512,1024]{1,0:T(8,128)}, f32[2,64,1024]{2,1,0:T(8,128)}) custom-call(s32[16]{0:T(128)} %owner.1, f32[4,4,64,1024]{3,2,1,0:T(8,128)} %bitcast.4, f32[512,1024]{1,0:T(8,128)} %bitcast.5), custom_call_target="tpu_custom_call" | custom-call | tf_op jit(solution)/shard_map/pallas_call | solution.py:571
  170.2 0.0 copy-start
  170.2 3.2 %copy.7 = f32[1,1,512,1024]{3,2,1,0:T(8,128)} copy(f32[1,1,512,1024]{3,2,1,0:T(8,128)} %bitcast.6) | data formatting | bytes 4194304
  173.4 0.0 copy-done
  173.4 0.8 copy.8
Async XLA Ops:
  170.2 3.2 %copy-start = (f32[2,64,1024]{2,1,0:T(8,128)S(1)}, f32[2,64,1024]{2,1,0:T(8,128)}, u32[]{:S(2)}) copy-start(f32[2,64,1024]{2,1,0:T(8,128)} %get-tuple-element.5) | copy-start | bytes 1572868

commit v3 on v2

--- a/solution.py
+++ b/solution.py
@@ -16,16 +16,18 @@
     ((0, 2), (0, 3), (0, 0), (0, 1), (1, 1)),
     ((2, 1), (3, 1), (2, 2), (2, 3), (3, 3)),
 )
-SETS = (pl.ds(0, 2), pl.ds(2, 3))
+OLD_SETS = (pl.ds(0, 2), pl.ds(2, 3))
+SETS = (pl.ds(0, 2), pl.ds(2, 2), pl.ds(4, 1))
 
 
 GRADS, OLD = 0, 1
 ORDER = (
-    (GRADS, 1, 0), (GRADS, 0, 2), (OLD, 2, 0), (GRADS, 1, 1), (GRADS, 2, 0), (OLD, 1, 1), (GRADS, 0, 3),
-    (GRADS, 1, 2), (GRADS, 3, 0), (GRADS, 2, 1), (GRADS, 4, 0), (OLD, 3, 0), (GRADS, 1, 3), (GRADS, 3, 1),
-    (GRADS, 2, 2), (GRADS, 5, 0), (GRADS, 4, 1), (OLD, 4, 0), (OLD, 2, 1), (GRADS, 2, 3), (GRADS, 3, 2),
-    (GRADS, 6, 0), (GRADS, 5, 1), (GRADS, 4, 2), (OLD, 5, 0), (OLD, 3, 1), (GRADS, 3, 3), (GRADS, 6, 1),
-    (GRADS, 5, 2), (GRADS, 4, 3), (OLD, 4, 1), (GRADS, 6, 2), (GRADS, 5, 3), (GRADS, 6, 3), (OLD, 5, 1),
+    (GRADS, 2, 0), (GRADS, 1, 1), (GRADS, 0, 2), (GRADS, 2, 1), (GRADS, 3, 0), (GRADS, 1, 2), (GRADS, 0, 3),
+    (GRADS, 2, 2), (GRADS, 4, 0), (GRADS, 3, 1), (GRADS, 1, 3), (OLD, 2, 0), (GRADS, 2, 3), (GRADS, 5, 0),
+    (GRADS, 4, 1), (GRADS, 3, 2), (OLD, 1, 1), (GRADS, 6, 0), (GRADS, 5, 1), (GRADS, 4, 2), (GRADS, 3, 3),
+    (OLD, 3, 0), (GRADS, 7, 0), (GRADS, 6, 1), (GRADS, 5, 2), (GRADS, 4, 3), (OLD, 4, 0), (OLD, 2, 1), (GRADS, 7, 1),
+    (GRADS, 6, 2), (GRADS, 5, 3), (OLD, 3, 1), (GRADS, 7, 2), (GRADS, 6, 3), (OLD, 5, 0), (OLD, 4, 1), (GRADS, 7, 3),
+    (OLD, 5, 1),
 )
 
 
@@ -112,30 +114,28 @@
 def top_value(stat, column):
 
     def to_column(row):
-        @pl.loop(0, 8)
-        def _(i):
-            rows = pl.ds(pl.multiple_of(i * 128, 128), 128)
+        for i in range(8):
+            rows = pl.ds(i * 128, 128)
             column[rows, :] = jnp.sum(stat[rows, :] * row, axis=1, keepdims=True)
-
         return column[...]
 
     def to_row(values):
         column[...] = values
-
-        def body(i, total):
-            rows = pl.ds(pl.multiple_of(i * 128, 128), 128)
-            return total + jnp.sum(stat[rows, :] * column[rows, :], axis=0, keepdims=True)
-
-        return lax.fori_loop(0, 8, body, jnp.zeros((1, BS), jnp.float32))
+        total = jnp.zeros((8, BS), jnp.float32)
+        for i in range(8):
+            rows = pl.ds(i * 128, 128)
+            total = total + jnp.sum((stat[rows, :] * column[rows, :]).reshape(16, 8, BS), axis=0)
+        return jnp.sum(total, axis=0, keepdims=True)
+
+    def norm(values):
+        return jnp.sqrt(jnp.sum(values * values, axis=(0, 1), keepdims=True))
 
     row = jnp.full((1, BS), BS ** (-0.5), jnp.float32)
     for _ in range(PSTEPS // 2):
         image = to_column(row)
-        image = image / jnp.sqrt(jnp.sum(image * image))
-        row = to_row(image)
-        row = row / jnp.sqrt(jnp.sum(row * row))
-    image = to_column(row)
-    return jnp.sqrt(jnp.sum(image * image, axis=(0, 1), keepdims=True))
+        row = to_row(image * (1.0 / norm(image)))
+        row = row * (1.0 / norm(row))
+    return norm(to_column(row))
 
 
 def find_root(spot, top, stat, root, base, high, low):
@@ -178,9 +178,9 @@
     packed, slots, oldp, both, chunk, gram, ggot, sall, stat, column, base, rootbuf = scratch[11:23]
     piece, parts, crossed, new = scratch[23:27]
     spread, outgo, income, near, cross, fin = (scratch[27 + 2 * n : 29 + 2 * n] for n in range(6))
-    columns, leave, enter, ready = (scratch[39 + 2 * n : 41 + 2 * n] for n in range(4))
-    mat_high, mat_low, high, low = scratch[47:51]
-    net = Network(*scratch[51:])
+    columns, leave, enter, ready = (scratch[39 + 3 * n : 42 + 3 * n] for n in range(4))
+    mat_high, mat_low, high, low = scratch[51:55]
+    net = Network(*scratch[55:])
     y, zl, x, zh, c = net.y, net.zl, net.x, net.zh, net.c
     side, half = zl // 2, zl % 2
     below, above, beyond = (y + 3) % 4, (y + 1) % 4, (y + 2) % 4
@@ -207,12 +207,15 @@
         + [dict(x=1), dict(x=2), dict(x=3), dict(zh=1), dict(c=1)]
     )
 
-    def scatter(group):
+    def scatter_far(group):
         far_up = net.push(strip(grads, beyond, 0, group), far.at[group, pl.ds(0, 2)], y=1)
         far_down = net.push(strip(grads, beyond, 2, group), far.at[group, pl.ds(2, 2)], y=3)
+        return far_up, far_down
+
+    def scatter_near(group, copies):
         near_up = net.push(strip(grads, above, 2, group), up.at[group, pl.ds(2, 2)], y=1)
         near_down = net.push(strip(grads, below, 0, group), down.at[group, pl.ds(0, 2)], y=3)
-        return far_up, far_down, near_up, near_down
+        return *copies, near_up, near_down
 
     def relay(group, copies):
         rows = pl.ds(group * SUB, SUB)
@@ -263,7 +266,7 @@
         return net.push(there, there, half=1), copies[1], copies[2]
 
     def start_old(n):
-        part = SETS[n]
+        part = OLD_SETS[n]
         own = net.move(packed.at[part, rows_of(y, 64)], slots.at[y, part])
         return own, {
             k: net.push(packed.at[part, rows_of((y + k) % 4, 64)], slots.at[y, part], y=k) for k in (1, 3, 2)
@@ -279,7 +282,7 @@
                 slotted[k].wait_recv()
             at = (y + 4 - k) % 4
             for m in (0, 1, 2, 3):
-                source = slots.at[at, SETS[n], rows_of((x + m) % 4, 16)]
+                source = slots.at[at, OLD_SETS[n], rows_of((x + m) % 4, 16)]
                 if m == 0:
                     local.append(net.move(source, spread[n].at[x * 4 + at]))
                 else:
@@ -307,7 +310,7 @@
         crossing.wait_recv()
         for i in range(4):
             fin[n][i] = near[n][i] + cross[n][i]
-        here = oldp.at[SETS[n], rows_of(x, 16)]
+        here = oldp.at[OLD_SETS[n], rows_of(x, 16)]
         own = net.move(fin[n].at[0], here)
         return own, [net.push(fin[n].at[m], here, x=m) for m in (1, 2, 3)]
 
@@ -322,13 +325,13 @@
         valid = (found == 1) & (source % 2 == c)
         return jnp.where(valid, source // 2, 0), jnp.where(valid, 1.0, 0.0)
 
-    stages = (scatter, relay, reduce_half, reduce_side, turn, gather_side, gather_half)
+    stages = (None, scatter_near, relay, reduce_half, reduce_side, turn, gather_side, gather_half)
     steps = (None, start_old, spread_old, swap_old, cross_old, finish_old)
     state, olds = {}, {}
 
     def run(stage, group):
         if stage == 0:
-            state[group] = scatter(group)
+            state[group] = scatter_far(group)
         else:
             state[group] = stages[stage](group, state[group])
 
@@ -339,10 +342,11 @@
             olds[n] = steps[step](n, olds[n])
 
     run(0, 0)
+    run(1, 0)
+    run(0, 1)
     for copy in fetched:
         copy.wait()
     run_old(1, 0)
-    run(0, 1)
     old_away = [lookup_old(n, 1 - c) for n in range(8)]
     old_home = [lookup_old(n, c) for n in range(8)]
     for copy in prefetch:
@@ -394,9 +398,10 @@
     own, across, first_up, first_down = [], [], [], []
     halved, y_up, y_down, y_far, other_up, other_down, other_far, own_piece = [], [], [], [], [], [], [], []
     for n, part in enumerate(SETS):
-        olds[n][0].wait()
-        for copy in olds[n][1]:
-            copy.wait_recv()
+        if n < 2:
+            olds[n][0].wait()
+            for copy in olds[n][1]:
+                copy.wait_recv()
         for copy in summed[n]:
             copy.wait_recv()
         piece[part] = 0.6 * oldp[part] + (1.0 - 0.6) * (
@@ -477,12 +482,28 @@
     start_other(1)
     pass_second(0)
     pass_other(0)
+    pass_first(2)
+    pass_own(2)
     start_second(1)
+    start_other(2)
     pass_other(1)
     sent = [choose(0)]
     pass_second(1)
-
-    for n in range(2):
+    start_second(2)
+    pass_other(2)
+    sent.append(choose(1))
+    pass_second(2)
+
+    halves = []
+    for k in (0, 1, 3, 2):
+        if k:
+            sent[0][0][k].wait_recv()
+        else:
+            sent[0][1].wait()
+        at = (y + 4 - k) % 4
+        halves.append(net.push(parts.at[SETS[0], at], crossed.at[:, at], half=1))
+
+    for n in range(3):
         own_piece[n].wait()
         for copy in (y_down[n], y_far[n], other_up[n], other_far[n]):
             copy.wait_recv()
@@ -493,23 +514,15 @@
     for i, j in ((0, 1), (0, 2), (0, 3), (2, 1), (3, 1), (2, 3)):
         stat[pl.ds(j * 256, 256), pl.ds(i * 256, 256)] = stat[pl.ds(i * 256, 256), pl.ds(j * 256, 256)].T
     top = top_value(stat, column)
-    sent.append(choose(1))
-
-    halves = []
-    for k in (0, 1, 3, 2):
-        if k:
-            sent[0][0][k].wait_recv()
-        else:
-            sent[0][1].wait()
-        at = (y + 4 - k) % 4
-        halves.append(net.push(parts.at[SETS[0], at], crossed.at[:, at], half=1))
+    sent.append(choose(2))
     find_root((y, zl), top, stat, rootbuf, base, high, low)
     returned = net.push(rootbuf.at[1], roots.at[side], side=1)
     kept = net.move(rootbuf.at[0], roots.at[side])
 
-    sent[1][1].wait()
-    for k in (1, 3, 2):
-        sent[1][0][k].wait_recv()
+    for n in (1, 2):
+        sent[n][1].wait()
+        for k in (1, 3, 2):
+            sent[n][0][k].wait_recv()
     for copy in halves:
         copy.wait_recv()
 
@@ -564,8 +577,10 @@
     scratch += [(2, GROUPS, 4, SUB, 256), (4, 4, 64, 256), (5, 256, 256), (3, *piece), (2, 5, 4, 64, 256)]
     scratch += [(BS, BS), (BS, 1), (BS, BS), (2, 64, BS)]
     scratch += [piece, (5, 4, 64, 256), (2, 4, 64, 256), (512, BS)]
-    for count, rows in ((16, 16), (8, 16), (8, 16), (8, 16), (4, 16), (4, 16), (8, 64), (4, 64), (4, 64), (4, 64)):
-        scratch += [(count, part.size, rows, 256) for part in SETS]
+    for count in (16, 8, 8, 8, 4, 4):
+        scratch += [(count, part.size, 16, 256) for part in OLD_SETS]
+    for count in (8, 4, 4, 4):
+        scratch += [(count, part.size, 64, 256) for part in SETS]
     halves = [(4, 256, 256), (4, 256, 256), (BS, BS), (BS, BS)]
     out_shape = (f32(512, BS), f32(2, 64, BS))
     return pl.pallas_call(
@@ -576,8 +591,8 @@
         scratch_shapes=[pltpu.VMEM(shape, jnp.float32) for shape in scratch]
         + [pltpu.VMEM(shape, jnp.bfloat16) for shape in halves]
         + [
-            pltpu.SemaphoreType.DMA((160,)),
-            pltpu.SemaphoreType.DMA((160,)),
+            pltpu.SemaphoreType.DMA((192,)),
+            pltpu.SemaphoreType.DMA((192,)),
             pltpu.SemaphoreType.DMA((48,)),
         ],
         compiler_params=pltpu.CompilerParams(

time: 178 us -> 170 us (0.955)
  Pallas kernels: 170 us -> 163 us
    pallas_call x1, Pallas kernels: 170 us -> 163 us  [refresh(): pl.pallas_call(refresh_kernel, out_shape=out_shape, in_specs=[pl.BlockSpe...]
where the time goes in v3:
time: 170 us; the launch traced here: 168 us
  Pallas kernels  163 us (96%)
  local copies, waits for them, and re-layouts  4.01 us (2%)
    pallas_call x1, Pallas kernels, refresh(): pl.pallas_call(refresh_kernel, out_shape=out_shape, in_specs=[pl.BlockSpe...  163 us
    unnamed x4, local copies, waits for them, and re-layouts  4.01 us

profile of v3, /device:TPU:4, one launch (start us, length us, event | category | flops | bytes accessed | tf_op | source)
XLA Modules:
  0.0 167.7 jit_solution(4106673573332019992)
XLA Ops:
  0.6 163.1 %shard_map.50 = (f32[512,1024]{1,0:T(8,128)}, f32[2,64,1024]{2,1,0:T(8,128)}) custom-call(s32[16]{0:T(128)} %owner.1, f32[4,4,64,1024]{3,2,1,0:T(8,128)} %bitcast.4, f32[512,1024]{1,0:T(8,128)} %bitcast.5), custom_call_target="tpu_custom_call" | custom-call | tf_op jit(solution)/shard_map/pallas_call | solution.py:586
  163.7 0.0 copy-start
  163.7 3.2 %copy.7 = f32[1,1,512,1024]{3,2,1,0:T(8,128)} copy(f32[1,1,512,1024]{3,2,1,0:T(8,128)} %bitcast.6) | data formatting | bytes 4194304
  166.9 0.0 copy-done
  166.9 0.8 copy.8
Async XLA Ops:
  163.7 3.2 %copy-start = (f32[2,64,1024]{2,1,0:T(8,128)S(1)}, f32[2,64,1024]{2,1,0:T(8,128)}, u32[]{:S(2)}) copy-start(f32[2,64,1024]{2,1,0:T(8,128)} %get-tuple-element.5) | copy-start | bytes 1572868

commit v4 on v3

--- a/solution.py
+++ b/solution.py
@@ -7,7 +7,7 @@
 
 PSTEPS = 8
 BS = 1024
-GROUPS = 4
+GROUPS = 8
 SUB = 64 // GROUPS
 MESH = pl.DeviceIdType.MESH
 VMEM_LIMIT = 60 * 1024 * 1024
@@ -22,12 +22,16 @@
 
 GRADS, OLD = 0, 1
 ORDER = (
-    (GRADS, 2, 0), (GRADS, 1, 1), (GRADS, 0, 2), (GRADS, 2, 1), (GRADS, 3, 0), (GRADS, 1, 2), (GRADS, 0, 3),
-    (GRADS, 2, 2), (GRADS, 4, 0), (GRADS, 3, 1), (GRADS, 1, 3), (OLD, 2, 0), (GRADS, 2, 3), (GRADS, 5, 0),
-    (GRADS, 4, 1), (GRADS, 3, 2), (OLD, 1, 1), (GRADS, 6, 0), (GRADS, 5, 1), (GRADS, 4, 2), (GRADS, 3, 3),
-    (OLD, 3, 0), (GRADS, 7, 0), (GRADS, 6, 1), (GRADS, 5, 2), (GRADS, 4, 3), (OLD, 4, 0), (OLD, 2, 1), (GRADS, 7, 1),
-    (GRADS, 6, 2), (GRADS, 5, 3), (OLD, 3, 1), (GRADS, 7, 2), (GRADS, 6, 3), (OLD, 5, 0), (OLD, 4, 1), (GRADS, 7, 3),
-    (OLD, 5, 1),
+    (OLD, 1, 0), (GRADS, 0, 2), (GRADS, 1, 2), (GRADS, 2, 0), (GRADS, 0, 3), (GRADS, 1, 3), (GRADS, 2, 1),
+    (OLD, 2, 0), (GRADS, 0, 4), (GRADS, 1, 4), (GRADS, 2, 2), (GRADS, 3, 0), (GRADS, 0, 5), (GRADS, 1, 5),
+    (GRADS, 2, 3), (OLD, 3, 0), (GRADS, 4, 0), (GRADS, 3, 1), (GRADS, 0, 6), (GRADS, 1, 6), (OLD, 4, 0),
+    (GRADS, 5, 0), (GRADS, 2, 4), (GRADS, 4, 1), (GRADS, 3, 2), (GRADS, 0, 7), (GRADS, 1, 7), (GRADS, 2, 5),
+    (GRADS, 3, 3), (OLD, 5, 0), (GRADS, 5, 1), (GRADS, 2, 6), (GRADS, 6, 0), (GRADS, 4, 2), (GRADS, 3, 4),
+    (GRADS, 4, 3), (GRADS, 7, 0), (GRADS, 2, 7), (GRADS, 5, 2), (OLD, 1, 1), (GRADS, 3, 5), (GRADS, 6, 1),
+    (GRADS, 4, 4), (GRADS, 3, 6), (GRADS, 5, 3), (GRADS, 3, 7), (GRADS, 6, 2), (GRADS, 4, 5), (GRADS, 7, 1),
+    (GRADS, 5, 4), (GRADS, 4, 6), (GRADS, 4, 7), (GRADS, 7, 2), (OLD, 2, 1), (GRADS, 6, 3), (GRADS, 6, 4),
+    (GRADS, 5, 5), (GRADS, 5, 6), (GRADS, 6, 5), (GRADS, 5, 7), (GRADS, 6, 6), (GRADS, 7, 3), (GRADS, 6, 7),
+    (GRADS, 7, 4), (GRADS, 7, 5), (OLD, 3, 1), (GRADS, 7, 6), (GRADS, 7, 7), (OLD, 4, 1), (OLD, 5, 1),
 )
 
 
@@ -344,9 +348,9 @@
     run(0, 0)
     run(1, 0)
     run(0, 1)
+    run(1, 1)
     for copy in fetched:
         copy.wait()
-    run_old(1, 0)
     old_away = [lookup_old(n, 1 - c) for n in range(8)]
     old_home = [lookup_old(n, c) for n in range(8)]
     for copy in prefetch:
@@ -591,9 +595,9 @@
         scratch_shapes=[pltpu.VMEM(shape, jnp.float32) for shape in scratch]
         + [pltpu.VMEM(shape, jnp.bfloat16) for shape in halves]
         + [
-            pltpu.SemaphoreType.DMA((192,)),
-            pltpu.SemaphoreType.DMA((192,)),
-            pltpu.SemaphoreType.DMA((48,)),
+            pltpu.SemaphoreType.DMA((256,)),
+            pltpu.SemaphoreType.DMA((256,)),
+            pltpu.SemaphoreType.DMA((64,)),
         ],
         compiler_params=pltpu.CompilerParams(
             collective_id=0, has_side_effects=True, vmem_limit_bytes=VMEM_LIMIT

time: 170 us -> 164 us (0.965)
  Pallas kernels: 163 us -> 158 us
    pallas_call x1, Pallas kernels: 163 us -> 158 us  [refresh(): pl.pallas_call(refresh_kernel, out_shape=out_shape, in_specs=[pl.BlockSpe...]
where the time goes in v4:
time: 164 us; the launch traced here: 163 us
  Pallas kernels  158 us (96%)
  local copies, waits for them, and re-layouts  4.01 us (2%)
    pallas_call x1, Pallas kernels, refresh(): pl.pallas_call(refresh_kernel, out_shape=out_shape, in_specs=[pl.BlockSpe...  158 us
    unnamed x4, local copies, waits for them, and re-layouts  4.01 us

profile of v4, /device:TPU:4, one launch (start us, length us, event | category | flops | bytes accessed | tf_op | source)
XLA Modules:
  0.0 162.6 jit_solution(12573030508912786982)
XLA Ops:
  0.6 158.0 %shard_map.50 = (f32[512,1024]{1,0:T(8,128)}, f32[2,64,1024]{2,1,0:T(8,128)}) custom-call(s32[16]{0:T(128)} %owner.1, f32[4,4,64,1024]{3,2,1,0:T(8,128)} %bitcast.4, f32[512,1024]{1,0:T(8,128)} %bitcast.5), custom_call_target="tpu_custom_call" | custom-call | tf_op jit(solution)/shard_map/pallas_call | solution.py:590
  158.6 0.0 copy-start
  158.6 3.2 %copy.7 = f32[1,1,512,1024]{3,2,1,0:T(8,128)} copy(f32[1,1,512,1024]{3,2,1,0:T(8,128)} %bitcast.6) | data formatting | bytes 4194304
  161.8 0.0 copy-done
  161.8 0.8 copy.8
Async XLA Ops:
  158.6 3.2 %copy-start = (f32[2,64,1024]{2,1,0:T(8,128)S(1)}, f32[2,64,1024]{2,1,0:T(8,128)}, u32[]{:S(2)}) copy-start(f32[2,64,1024]{2,1,0:T(8,128)} %get-tuple-element.5) | copy-start | bytes 1572868

commit v5 on v4

--- a/solution.py
+++ b/solution.py
@@ -399,7 +399,7 @@
             ]
         )
     back, on = (x + 3) % 4, (x + 1) % 4
-    own, across, first_up, first_down = [], [], [], []
+    own, across, first_up, first_down = [], {}, [], []
     halved, y_up, y_down, y_far, other_up, other_down, other_far, own_piece = [], [], [], [], [], [], [], []
     for n, part in enumerate(SETS):
         if n < 2:
@@ -413,7 +413,8 @@
         )
         here, there = columns[n].at[x * 2 + zh], sall.at[half, part, y]
         halved.append(net.push(piece.at[part], there, half=1))
-        across.append(net.push(piece.at[part], here, zh=1))
+        for late in ((0,), (), (1, 2))[n]:
+            across[late] = net.push(piece.at[SETS[late]], columns[late].at[x * 2 + zh], zh=1)
         first_up.append(net.push(piece.at[part], here, x=1))
         first_down.append(net.push(piece.at[part], here, x=3))
         y_up.append(net.push(piece.at[part], there, y=1))

time: 164 us -> 164 us (level)
  no operation moved by 1% of the time
where the time goes in v5:
time: 164 us; the launch traced here: 163 us
  Pallas kernels  158 us (96%)
  local copies, waits for them, and re-layouts  4.01 us (2%)
    pallas_call x1, Pallas kernels, refresh(): pl.pallas_call(refresh_kernel, out_shape=out_shape, in_specs=[pl.BlockSpe...  158 us
    unnamed x4, local copies, waits for them, and re-layouts  4.01 us

profile of v5, /device:TPU:4, one launch (start us, length us, event | category | flops | bytes accessed | tf_op | source)
XLA Modules:
  0.0 162.7 jit_solution(13734972172592651649)
XLA Ops:
  0.6 158.1 %shard_map.50 = (f32[512,1024]{1,0:T(8,128)}, f32[2,64,1024]{2,1,0:T(8,128)}) custom-call(s32[16]{0:T(128)} %owner.1, f32[4,4,64,1024]{3,2,1,0:T(8,128)} %bitcast.4, f32[512,1024]{1,0:T(8,128)} %bitcast.5), custom_call_target="tpu_custom_call" | custom-call | tf_op jit(solution)/shard_map/pallas_call | solution.py:591
  158.7 0.0 copy-start
  158.7 3.2 %copy.7 = f32[1,1,512,1024]{3,2,1,0:T(8,128)} copy(f32[1,1,512,1024]{3,2,1,0:T(8,128)} %bitcast.6) | data formatting | bytes 4194304
  161.9 0.0 copy-done
  161.9 0.8 copy.8
Async XLA Ops:
  158.7 3.2 %copy-start = (f32[2,64,1024]{2,1,0:T(8,128)S(1)}, f32[2,64,1024]{2,1,0:T(8,128)}, u32[]{:S(2)}) copy-start(f32[2,64,1024]{2,1,0:T(8,128)} %get-tuple-element.5) | copy-start | bytes 1572868
